TPU v7x, 32 devices: a whole 2x2x4 slice. The times are simulated.
32 devices in a mesh: fsdp: 32 (over z, y, x, core).
Axes of the slice: x: 2, y: 2, z: 4, core: 2. Of those that a mesh axis runs over, the one named last changes fastest.
Arguments:
- block_input: bfloat16 [4096, 1024], P('fsdp'), may hold values from -6 to 6
- seq_lengths: int32 [48], replicated, may hold values from 32 to 64, as said below
- seq_devices: int32 [48], replicated, may hold values from 0 to 31, as said below
- expert_ids: int32 [4096, 8], P('fsdp'), may hold values from 0 to 31, all different within a row; in each aligned block of 128 rows (0 to 127, 128 to 255, ...) at most 40 rows name the same one
- attn_gain: bfloat16 [1024], P('fsdp'), may hold values from 0.5 to 1.5
- query_weight: bfloat16 [1024, 1024], P('fsdp'), may hold values from -0.1875 to 0.1875
- keyvalue_weight: bfloat16 [1024, 1024], P('fsdp'), may hold values from -0.1875 to 0.1875
- output_weight: bfloat16 [1024, 1024], P('fsdp'), may hold values from -1 to 1
- moe_gain: bfloat16 [1024], P('fsdp'), may hold values from 0.5 to 1.5
- router_weight: bfloat16 [1024, 32], P('fsdp'), may hold values from -0.09375 to 0.09375
- gate_weight: bfloat16 [16384, 1024], P('fsdp'), may hold values from -0.1875 to 0.1875
- up_weight: bfloat16 [16384, 1024], P('fsdp'), may hold values from -0.1875 to 0.1875
- down_weight: bfloat16 [16384, 1024], P('fsdp'), may hold values from -0.75 to 0.75
- output_grad: bfloat16 [4096, 1024], P('fsdp'), may hold values from -6 to 6
Outputs:
- block_output: bfloat16 [4096, 1024], P('fsdp')
- input_grad: float32 [4096, 1024], P('fsdp')
- attn_gain_grad: float32 [1024], P('fsdp')
- query_grad: float32 [1024, 1024], P('fsdp')
- keyvalue_grad: float32 [1024, 1024], P('fsdp')
- output_weight_grad: float32 [1024, 1024], P('fsdp')
- moe_gain_grad: float32 [1024], P('fsdp')
- router_grad: float32 [1024, 32], P('fsdp')
- gate_grad: float32 [16384, 1024], P('fsdp')
- up_grad: float32 [16384, 1024], P('fsdp')
- down_grad: float32 [16384, 1024], P('fsdp')
Inputs may be any that keep to these rules, and one draw needn't show every extreme that they name: `seq_lengths`: no device holds more than 2 sequences, so one device's lengths sum to 128 or less; in every draw one device holds 2 sequences of 64 rows. `seq_devices`: no device index is named more than 2 times; one is named exactly 2 times. `expert_ids`: each row names 8 different experts. Within the rows of one device no expert is named by more than 40 rows, and in some device's rows one expert is named by exactly 40.
All inputs are finite; a program needn't handle non-finite values.
Results may differ from a plain program's by a relative error of at most 0.013.
The roundings to bfloat16 on the way count: a program that leaves them out, or rounds other values in their place, can miss the bound.
Values may be sent and summed in bfloat16 or wider, within the bound.
No kernel may reach another device: no remote copies, remote signals or barrier semaphores. Data moves between devices by JAX's collectives and lax.ppermute only.
A program may use at most 640 MiB of HBM per device.

v0:
```python
from functools import partial

import jax
import jax.numpy as jnp
from jax import lax
from jax.sharding import PartitionSpec as P

QUERY_HEADS = 16
KEY_VALUE_HEADS = 8
HEAD_WIDTH = 64
EXPERT_COUNT = 32
EXPERT_HIDDEN = 512
TOPK = 8
CAP = 40


EPS = 1e-06
ROPE_BASE = 10000.0


def layout(seq_lengths, seq_devices, device, count_of_rows):
    on_device = seq_devices == device
    lengths = jnp.where(on_device, seq_lengths, 0)
    starts = jnp.cumsum(lengths) - lengths
    filled_rows = jnp.sum(lengths)
    row_slots = jnp.arange(count_of_rows, dtype=jnp.int32)
    inside = (row_slots[:, None] >= starts[None, :]) & (
        row_slots[:, None] < (starts + lengths)[None, :]
    )
    live_rows = jnp.any(inside, axis=1)
    seq_count = seq_lengths.shape[0]
    numbers = jnp.arange(seq_count, dtype=jnp.int32)
    segment = jnp.where(
        live_rows, jnp.sum(jnp.where(inside, numbers[None, :], 0), axis=1), seq_count
    )
    begins = jnp.where(
        live_rows, jnp.sum(jnp.where(inside, starts[None, :], 0), axis=1), filled_rows
    )
    return (live_rows, segment, row_slots - begins)


def rope_tables(position, head_dim):
    half_dim = head_dim // 2
    inverse = ROPE_BASE ** (-(jnp.arange(half_dim, dtype=jnp.float32) * 2.0) / head_dim)
    angles = position.astype(jnp.float32)[:, None] * inverse[None, :]
    return (jnp.cos(angles)[:, None, :], jnp.sin(angles)[:, None, :])


def rotate(values, cosine, sine_part, head_dim):
    count_of_rows = values.shape[0]
    shaped = values.reshape(count_of_rows, -1, head_dim)
    half_dim = head_dim // 2
    first_half = shaped[..., :half_dim]
    second_half = shaped[..., half_dim:]
    turned = jnp.concatenate(
        [
            first_half * cosine - second_half * sine_part,
            second_half * cosine + first_half * sine_part,
        ],
        axis=-1,
    )
    return turned.reshape(count_of_rows, -1)


def norm_forward(hidden, gain_vec):
    inv_rms = lax.rsqrt(jnp.mean(hidden * hidden, axis=-1, keepdims=True) + EPS)
    unit_rows = hidden * inv_rms
    return (unit_rows * gain_vec.astype(jnp.float32), unit_rows, inv_rms)


def norm_backward(grad_norm, gain_vec, unit_rows, inv_rms):
    grad_unit = grad_norm * gain_vec.astype(jnp.float32)
    grad_gain = jnp.sum(grad_norm * unit_rows, axis=0)
    grad_hidden = inv_rms * (
        grad_unit - unit_rows * jnp.mean(grad_unit * unit_rows, axis=-1, keepdims=True)
    )
    return (grad_hidden, grad_gain)


def dispatch(expert_ids, experts, capacity):
    count_of_rows, top_count = expert_ids.shape
    flat_ids = expert_ids.reshape(-1)
    one_hot = (flat_ids[:, None] == jnp.arange(experts, dtype=jnp.int32)[None, :]).astype(jnp.int32)
    earlier = jnp.cumsum(one_hot, axis=0) - one_hot
    order_in = jnp.sum(earlier * one_hot, axis=1)
    pair_slot = flat_ids * capacity + order_in
    pair_token = jnp.arange(count_of_rows * top_count, dtype=jnp.int32) // top_count
    slot_token = jnp.zeros((experts * capacity,), jnp.int32).at[pair_slot].set(pair_token)
    slot_used = jnp.zeros((experts * capacity,), jnp.int32).at[pair_slot].set(1) > 0
    return (pair_slot, slot_token, slot_used)


def head_forward(operands, allowed):
    query_rows, keys_head, values_head = operands
    scale_factor = query_rows.shape[-1] ** (-0.5)
    scores = (
        jnp.einsum("qgd,kd->gqk", query_rows, keys_head, preferred_element_type=jnp.float32)
        * scale_factor
    )
    scores = jnp.where(allowed[None], scores, -jnp.inf)
    highest = jnp.max(scores, axis=-1, keepdims=True)
    totals = jnp.sum(jnp.exp(scores - highest), axis=-1, keepdims=True)
    log_total = highest + jnp.log(totals)
    prob_bf = jnp.exp(scores - log_total).astype(jnp.bfloat16)
    mixed_out = jnp.einsum(
        "gqk,kd->qgd", prob_bf, values_head, preferred_element_type=jnp.float32
    ).astype(jnp.bfloat16)
    return (mixed_out, log_total[..., 0])


def head_backward(operands, allowed):
    query_rows, keys_head, values_head, mixed_out, grad_mixed, log_total = operands
    scale_factor = query_rows.shape[-1] ** (-0.5)
    scores = (
        jnp.einsum("qgd,kd->gqk", query_rows, keys_head, preferred_element_type=jnp.float32)
        * scale_factor
    )
    prob_full = jnp.where(allowed[None], jnp.exp(scores - log_total[..., None]), 0.0)
    prob_bf = prob_full.astype(jnp.bfloat16)
    grad_values = jnp.einsum("gqk,qgd->kd", prob_bf, grad_mixed, preferred_element_type=jnp.float32)
    grad_probs = jnp.einsum(
        "qgd,kd->gqk", grad_mixed, values_head, preferred_element_type=jnp.float32
    )
    inner = jnp.sum(
        grad_mixed.astype(jnp.float32) * mixed_out.astype(jnp.float32), axis=-1
    ).transpose(1, 0)
    grad_scores = (prob_full * (grad_probs - inner[..., None])).astype(jnp.bfloat16)
    grad_queries = (
        jnp.einsum("gqk,kd->qgd", grad_scores, keys_head, preferred_element_type=jnp.float32)
        * scale_factor
    )
    grad_keys = (
        jnp.einsum("gqk,qgd->kd", grad_scores, query_rows, preferred_element_type=jnp.float32)
        * scale_factor
    )
    return (grad_queries, grad_keys, grad_values)


def body(
    block_input,
    seq_lengths,
    seq_devices,
    expert_ids,
    attn_gain,
    query_weight,
    keyvalue_weight,
    output_weight,
    moe_gain,
    router_weight,
    gate_weight,
    up_weight,
    down_weight,
    output_grad,
):
    count_of_rows, model_width = block_input.shape
    device = lax.axis_index("fsdp")
    shard_rows = gate_weight.shape[0]
    query_group_width = QUERY_HEADS // KEY_VALUE_HEADS
    key_value_columns = KEY_VALUE_HEADS * HEAD_WIDTH
    zero_index = jnp.zeros((), jnp.int32)
    live_rows, segment, position = layout(seq_lengths, seq_devices, device, count_of_rows)
    row_slots = jnp.arange(count_of_rows, dtype=jnp.int32)
    allowed = (segment[:, None] == segment[None, :]) & (row_slots[:, None] >= row_slots[None, :])
    cosine, sine_part = rope_tables(position, HEAD_WIDTH)
    full_gain1, full_query, full_kv, full_out, full_gain2, full_router = (
        lax.all_gather(attn_gain, "fsdp", axis=0, tiled=True),
        lax.all_gather(query_weight, "fsdp", axis=0, tiled=True),
        lax.all_gather(keyvalue_weight, "fsdp", axis=0, tiled=True),
        lax.all_gather(output_weight, "fsdp", axis=0, tiled=True),
        lax.all_gather(moe_gain, "fsdp", axis=0, tiled=True),
        lax.all_gather(router_weight, "fsdp", axis=0, tiled=True),
    )
    input_f = block_input.astype(jnp.float32)
    attn_norm, attn_unit, attn_rms = norm_forward(input_f, full_gain1)
    attn_in = attn_norm.astype(jnp.bfloat16)
    query_pre = jnp.dot(attn_in, full_query, preferred_element_type=jnp.float32)
    kv_pre = jnp.dot(attn_in, full_kv, preferred_element_type=jnp.float32)
    query_rows = rotate(query_pre, cosine, sine_part, HEAD_WIDTH).astype(jnp.bfloat16)
    gathered_keys = rotate(kv_pre[:, :key_value_columns], cosine, sine_part, HEAD_WIDTH).astype(
        jnp.bfloat16
    )
    gathered_values = kv_pre[:, key_value_columns:].astype(jnp.bfloat16)
    query_head_rows = query_rows.reshape(
        count_of_rows, KEY_VALUE_HEADS, query_group_width, HEAD_WIDTH
    ).transpose(1, 0, 2, 3)
    key_head_rows = gathered_keys.reshape(count_of_rows, KEY_VALUE_HEADS, HEAD_WIDTH).transpose(
        1, 0, 2
    )
    value_head_rows = gathered_values.reshape(count_of_rows, KEY_VALUE_HEADS, HEAD_WIDTH).transpose(
        1, 0, 2
    )
    mixed_heads, log_totals = lax.map(
        partial(head_forward, allowed=allowed), (query_head_rows, key_head_rows, value_head_rows)
    )
    attn_heads = mixed_heads.transpose(1, 0, 2, 3).reshape(count_of_rows, QUERY_HEADS * HEAD_WIDTH)
    residual = input_f + jnp.dot(attn_heads, full_out, preferred_element_type=jnp.float32)
    moe_norm, moe_unit, moe_rms = norm_forward(residual, full_gain2)
    moe_in = moe_norm.astype(jnp.bfloat16)
    logits = jnp.dot(moe_in, full_router, preferred_element_type=jnp.float32)
    picker = expert_ids[:, :, None] == jnp.arange(EXPERT_COUNT, dtype=jnp.int32)[None, None, :]
    chosen = jnp.sum(jnp.where(picker, logits[:, None, :], 0.0), axis=-1)
    raised = jnp.exp(chosen)
    route_weights = raised / jnp.sum(raised, axis=-1, keepdims=True)
    pair_slot, slot_token, slot_used = dispatch(expert_ids, EXPERT_COUNT, CAP)
    slot_inputs = jnp.where(
        slot_used[:, None], moe_in[slot_token], jnp.zeros((), jnp.bfloat16)
    ).reshape(EXPERT_COUNT, CAP, model_width)
    forward_init = (
        jnp.zeros((EXPERT_COUNT, CAP, model_width), jnp.float32),
        jnp.zeros((EXPERT_COUNT, CAP, EXPERT_HIDDEN), jnp.float32),
        jnp.zeros((EXPERT_COUNT, CAP, EXPERT_HIDDEN), jnp.float32),
        jnp.zeros((EXPERT_COUNT, CAP, EXPERT_HIDDEN), jnp.bfloat16),
    )
    piece_gate = lax.all_gather(gate_weight, "fsdp", axis=0, tiled=True)
    piece_up = lax.all_gather(up_weight, "fsdp", axis=0, tiled=True)
    piece_down = lax.all_gather(down_weight, "fsdp", axis=0, tiled=True)

    def forward_one_block(block_idx, inner_state):
        out_acc, gate_acc, up_acc, act_acc = inner_state
        offset = block_idx * shard_rows
        expert = offset // EXPERT_HIDDEN
        column = offset % EXPERT_HIDDEN
        rows_gate = lax.dynamic_slice_in_dim(piece_gate, offset, shard_rows, 0)
        rows_up = lax.dynamic_slice_in_dim(piece_up, offset, shard_rows, 0)
        rows_down = lax.dynamic_slice_in_dim(piece_down, offset, shard_rows, 0)
        inputs_e = lax.dynamic_index_in_dim(slot_inputs, expert, 0, keepdims=False)
        gate_pre = jnp.einsum("cd,hd->ch", inputs_e, rows_gate, preferred_element_type=jnp.float32)
        up_pre = jnp.einsum("cd,hd->ch", inputs_e, rows_up, preferred_element_type=jnp.float32)
        activation = (jax.nn.silu(gate_pre) * up_pre).astype(jnp.bfloat16)
        part_out = jnp.dot(activation, rows_down, preferred_element_type=jnp.float32)
        out_acc = out_acc.at[expert].add(part_out)
        corner = (expert, zero_index, column)
        gate_acc = lax.dynamic_update_slice(gate_acc, gate_pre[None], corner)
        up_acc = lax.dynamic_update_slice(up_acc, up_pre[None], corner)
        act_acc = lax.dynamic_update_slice(act_acc, activation[None], corner)
        return (out_acc, gate_acc, up_acc, act_acc)

    slot_outputs, slot_gates, slot_ups, slot_acts = lax.fori_loop(
        0, piece_gate.shape[0] // shard_rows, forward_one_block, forward_init
    )
    picked = slot_outputs.reshape(EXPERT_COUNT * CAP, model_width)[pair_slot].reshape(
        count_of_rows, TOPK, model_width
    )
    moe_out = jnp.sum(route_weights[:, :, None] * picked, axis=1)
    live_col = live_rows[:, None]
    block_output = jnp.where(live_col, residual + moe_out, 0.0).astype(jnp.bfloat16)
    out_cot = jnp.where(live_col, output_grad.astype(jnp.float32), 0.0)
    route_grad = jnp.sum(out_cot[:, None, :] * picked, axis=-1)
    chosen_grad = route_weights * (
        route_grad - jnp.sum(route_weights * route_grad, axis=-1, keepdims=True)
    )
    logit_grad = jnp.sum(jnp.where(picker, chosen_grad[:, :, None], 0.0), axis=1).astype(
        jnp.bfloat16
    )
    slot_weight = (
        jnp.zeros((EXPERT_COUNT * CAP,), jnp.float32).at[pair_slot].set(route_weights.reshape(-1))
    )
    slot_cot = (
        jnp.where(slot_used[:, None], out_cot[slot_token] * slot_weight[:, None], 0.0)
        .astype(jnp.bfloat16)
        .reshape(EXPERT_COUNT, CAP, model_width)
    )
    back_gain1, back_query, back_kv, back_out, back_gain2, back_router = (
        lax.all_gather(attn_gain, "fsdp", axis=0, tiled=True),
        lax.all_gather(query_weight, "fsdp", axis=0, tiled=True),
        lax.all_gather(keyvalue_weight, "fsdp", axis=0, tiled=True),
        lax.all_gather(output_weight, "fsdp", axis=0, tiled=True),
        lax.all_gather(moe_gain, "fsdp", axis=0, tiled=True),
        lax.all_gather(router_weight, "fsdp", axis=0, tiled=True),
    )
    backward_init = (
        jnp.zeros((EXPERT_COUNT, CAP, model_width), jnp.float32),
        jnp.zeros((EXPERT_COUNT, CAP, EXPERT_HIDDEN), jnp.bfloat16),
        jnp.zeros((EXPERT_COUNT, CAP, EXPERT_HIDDEN), jnp.bfloat16),
    )
    backward_piece_gate = lax.all_gather(gate_weight, "fsdp", axis=0, tiled=True)
    backward_piece_up = lax.all_gather(up_weight, "fsdp", axis=0, tiled=True)
    backward_piece_down = lax.all_gather(down_weight, "fsdp", axis=0, tiled=True)

    def backward_one_block(block_idx, inner_state):
        grad_acc, ggate_acc, gup_acc = inner_state
        offset = block_idx * shard_rows
        expert = offset // EXPERT_HIDDEN
        column = offset % EXPERT_HIDDEN
        corner = (expert, zero_index, column)
        rows_gate = lax.dynamic_slice_in_dim(backward_piece_gate, offset, shard_rows, 0)
        rows_up = lax.dynamic_slice_in_dim(backward_piece_up, offset, shard_rows, 0)
        rows_down = lax.dynamic_slice_in_dim(backward_piece_down, offset, shard_rows, 0)
        cot_e = lax.dynamic_index_in_dim(slot_cot, expert, 0, keepdims=False)
        gate_e = lax.dynamic_slice(slot_gates, corner, (1, CAP, shard_rows))[0]
        up_e = lax.dynamic_slice(slot_ups, corner, (1, CAP, shard_rows))[0]
        act_grad = jnp.einsum("cd,hd->ch", cot_e, rows_down, preferred_element_type=jnp.float32)
        sigma = jax.nn.sigmoid(gate_e)
        gate_pre_grad = (act_grad * up_e * sigma * (1.0 + gate_e * (1.0 - sigma))).astype(
            jnp.bfloat16
        )
        up_pre_grad = (act_grad * gate_e * sigma).astype(jnp.bfloat16)
        part_in = jnp.dot(gate_pre_grad, rows_gate, preferred_element_type=jnp.float32) + jnp.dot(
            up_pre_grad, rows_up, preferred_element_type=jnp.float32
        )
        grad_acc = grad_acc.at[expert].add(part_in)
        ggate_acc = lax.dynamic_update_slice(ggate_acc, gate_pre_grad[None], corner)
        gup_acc = lax.dynamic_update_slice(gup_acc, up_pre_grad[None], corner)
        return (grad_acc, ggate_acc, gup_acc)

    slot_in_grads, slot_ggates, slot_gups = lax.fori_loop(
        0, backward_piece_gate.shape[0] // shard_rows, backward_one_block, backward_init
    )

    def one_term(block_idx):
        row_start = block_idx * shard_rows
        expert = row_start // EXPERT_HIDDEN
        column = row_start % EXPERT_HIDDEN
        corner = (expert, zero_index, column)
        inputs_e = lax.dynamic_index_in_dim(slot_inputs, expert, 0, keepdims=False)
        cot_e = lax.dynamic_index_in_dim(slot_cot, expert, 0, keepdims=False)
        ggate_e = lax.dynamic_slice(slot_ggates, corner, (1, CAP, shard_rows))[0]
        gup_e = lax.dynamic_slice(slot_gups, corner, (1, CAP, shard_rows))[0]
        act_e = lax.dynamic_slice(slot_acts, corner, (1, CAP, shard_rows))[0]
        return jnp.concatenate(
            [
                jnp.einsum("ch,cd->hd", ggate_e, inputs_e, preferred_element_type=jnp.float32),
                jnp.einsum("ch,cd->hd", gup_e, inputs_e, preferred_element_type=jnp.float32),
                jnp.einsum("ch,cd->hd", act_e, cot_e, preferred_element_type=jnp.float32),
            ],
            axis=1,
        )

    blocks = lax.map(
        one_term, jnp.arange(lax.axis_size("fsdp") * shard_rows // shard_rows, dtype=jnp.int32)
    )
    expert_terms = lax.psum_scatter(
        blocks.reshape(lax.axis_size("fsdp") * shard_rows, 3 * model_width),
        "fsdp",
        scatter_dimension=0,
        tiled=True,
    )
    gate_grad = expert_terms[:, :model_width]
    up_grad = expert_terms[:, model_width : 2 * model_width]
    down_grad = expert_terms[:, 2 * model_width :]
    in_grads_flat = slot_in_grads.reshape(EXPERT_COUNT * CAP, model_width)
    moe_in_grad = jnp.sum(
        in_grads_flat[pair_slot].reshape(count_of_rows, TOPK, model_width), axis=1
    ) + jnp.einsum("te,de->td", logit_grad, back_router, preferred_element_type=jnp.float32)
    router_grad = jnp.einsum("td,te->de", moe_in, logit_grad, preferred_element_type=jnp.float32)
    resid_part, moe_gain_grad = norm_backward(moe_in_grad, back_gain2, moe_unit, moe_rms)
    residual_grad = out_cot + resid_part
    residual_bf = residual_grad.astype(jnp.bfloat16)
    output_weight_grad = jnp.einsum(
        "tf,td->fd", attn_heads, residual_bf, preferred_element_type=jnp.float32
    )
    gradient_per_head = jnp.einsum(
        "td,fd->tf", residual_bf, back_out, preferred_element_type=jnp.float32
    ).astype(jnp.bfloat16)
    head_gradients = gradient_per_head.reshape(
        count_of_rows, KEY_VALUE_HEADS, query_group_width, HEAD_WIDTH
    ).transpose(1, 0, 2, 3)
    grad_q, grad_k, grad_v = lax.map(
        partial(head_backward, allowed=allowed),
        (query_head_rows, key_head_rows, value_head_rows, mixed_heads, head_gradients, log_totals),
    )
    query_rot_grad = grad_q.transpose(1, 0, 2, 3).reshape(count_of_rows, QUERY_HEADS * HEAD_WIDTH)
    key_rot_grad = grad_k.transpose(1, 0, 2).reshape(count_of_rows, key_value_columns)
    value_grad = grad_v.transpose(1, 0, 2).reshape(count_of_rows, key_value_columns)
    query_pre_grad = rotate(query_rot_grad, cosine, -sine_part, HEAD_WIDTH).astype(jnp.bfloat16)
    kv_pre_grad = jnp.concatenate(
        [rotate(key_rot_grad, cosine, -sine_part, HEAD_WIDTH), value_grad], axis=1
    ).astype(jnp.bfloat16)
    query_grad = jnp.einsum(
        "td,tf->df", attn_in, query_pre_grad, preferred_element_type=jnp.float32
    )
    keyvalue_grad = jnp.einsum(
        "td,tf->df", attn_in, kv_pre_grad, preferred_element_type=jnp.float32
    )
    attn_in_grad = jnp.einsum(
        "tf,df->td", query_pre_grad, back_query, preferred_element_type=jnp.float32
    ) + jnp.einsum("tf,df->td", kv_pre_grad, back_kv, preferred_element_type=jnp.float32)
    input_part, attn_gain_grad = norm_backward(attn_in_grad, back_gain1, attn_unit, attn_rms)
    input_grad = jnp.where(live_col, residual_grad + input_part, 0.0)
    dense_sums = (
        lax.psum_scatter(attn_gain_grad, "fsdp", scatter_dimension=0, tiled=True),
        lax.psum_scatter(query_grad, "fsdp", scatter_dimension=0, tiled=True),
        lax.psum_scatter(keyvalue_grad, "fsdp", scatter_dimension=0, tiled=True),
        lax.psum_scatter(output_weight_grad, "fsdp", scatter_dimension=0, tiled=True),
        lax.psum_scatter(moe_gain_grad, "fsdp", scatter_dimension=0, tiled=True),
        lax.psum_scatter(router_grad, "fsdp", scatter_dimension=0, tiled=True),
    )
    return (
        block_output,
        input_grad,
        dense_sums[0],
        dense_sums[1],
        dense_sums[2],
        dense_sums[3],
        dense_sums[4],
        dense_sums[5],
        gate_grad,
        up_grad,
        down_grad,
    )


def solution(mesh):
    placed = (
        P("fsdp", None),
        P(),
        P(),
        P("fsdp", None),
        P("fsdp"),
        P("fsdp", None),
        P("fsdp", None),
        P("fsdp", None),
        P("fsdp"),
        P("fsdp", None),
        P("fsdp", None),
        P("fsdp", None),
        P("fsdp", None),
        P("fsdp", None),
    )
    return jax.shard_map(
        body,
        mesh=mesh,
        in_specs=placed,
        out_specs=(
            P("fsdp", None),
            P("fsdp", None),
            P("fsdp"),
            P("fsdp", None),
            P("fsdp", None),
            P("fsdp", None),
            P("fsdp"),
            P("fsdp", None),
            P("fsdp", None),
            P("fsdp", None),
            P("fsdp", None),
        ),
        check_vma=False,
    )
```

profile of v0, /device:TPU:0, one launch (start us, length us, event | category | flops | bytes accessed | tf_op | source)
XLA Modules:
  0.0 3733.7 jit_solution(2503168554658976032)
XLA Ops:
  12.1 42.2 %all-reduce.5 = (bf16[1024]{0:T(1024)(128)(2,1)S(1)}, bf16[1024]{0:T(1024)(128)(2,1)S(1)}) all-reduce(bf16[1024]{0:T(1024)(128)(2,1)S(1)} %dynamic-update-slice.20, bf16[1024]{0:T(1024)(128)(2,1)S(1)} %dynamic-update-slice.21), channel_id=1, replica_groups=mesh['fsdp'=32] {'fsdp'}, use_global_device_ids=true, to_apply=%add | all-reduce | flops 2048 | bytes 8192
  55.4 9.0 reduce-window.19
  74.0 5.1 gather_fusion.2
  79.1 41.1 %all_gather.41 = bf16[1024,32]{1,0:T(8,128)(2,1)S(1)} all-gather(bf16[32,32]{1,0:T(8,128)(2,1)S(1)} %copy-done.9), channel_id=1, replica_groups=mesh['fsdp'=32] {'fsdp'}, dimensions={0}, use_global_device_ids=true | all-gather | bytes 67584 | tf_op jit(solution)/shard_map/all_gather | solution.py:171
  123.8 4.5 all-gather.9.cloned.1.call-done
  135.4 51.0 %all-gather.11.cloned.1.call-done = bf16[1024,1024]{1,0:T(8,128)(2,1)} async-done(((bf16[32,1024]{1,0:T(8,128)(2,1)}), bf16[1024,1024]{1,0:T(8,128)(2,1)}) %all-gather.11.cloned.1.call-update) | async-done | bytes 2097168 | tf_op jit(solution)/shard_map/all_gather | solution.py:169
  188.7 5.1 gather_fusion
  206.3 176.5 %all-gather.13.cloned.1.call-done = bf16[16384,1024]{1,0:T(8,128)(2,1)} async-done(((bf16[512,1024]{1,0:T(8,128)(2,1)}), bf16[16384,1024]{1,0:T(8,128)(2,1)}) %all-gather.13.cloned.1.call-update) | async-done | bytes 33554448 | tf_op jit(solution)/shard_map/all_gather | solution.py:214
  382.8 195.7 %all-gather.15.cloned.1.call-done = bf16[16384,1024]{1,0:T(8,128)(2,1)} async-done(((bf16[512,1024]{1,0:T(8,128)(2,1)}), bf16[16384,1024]{1,0:T(8,128)(2,1)}) %all-gather.15.cloned.1.call-update) | async-done | bytes 33554448 | tf_op jit(solution)/shard_map/all_gather | solution.py:215
  578.5 195.7 %all-gather.17.cloned.1.call-done = bf16[16384,1024]{1,0:T(8,128)(2,1)} async-done(((bf16[512,1024]{1,0:T(8,128)(2,1)}), bf16[16384,1024]{1,0:T(8,128)(2,1)}) %all-gather.17.cloned.1.call-update) | async-done | bytes 33554448 | tf_op jit(solution)/shard_map/all_gather | solution.py:216
  782.0 282.6 %while.82 = (s32[]{:T(128)}, f32[32,40,1024]{2,1,0:T(8,128)}, f32[32,40,512]{2,1,0:T(8,128)}, f32[32,40,512]{2,1,0:T(8,128)}, bf16[32,40,512]{2,1,0:T(8,128)(2,1...) while((s32[]{:T(128)}, f32[32,40,1024]{2,1,0:T(8,128)}, ...), condition=%wide.region_20.21_spmd, body=%wide.region_18.20_spmd.sunk | while | flops 126033960 | bytes 4255659 | solution.py:238
  1069.9 236.3 %while.83 = (s32[]{:T(128)}, f32[32,40,1024]{2,1,0:T(8,128)}, bf16[32,40,512]{2,1,0:T(8,128)(2,1)}, bf16[32,40,512]{2,1,0:T(8,128)(2,1)}, bf16[32,40,1024]{2,1,0...) while((s32[]{:T(128)}, f32[32,40,1024]{2,1,0:T(8,128)}, ...), condition=%wide.region_25.26_spmd, body=%wide.region_23.25_spmd.sunk | while | flops 126218280 | bytes 4295091 | solution.py:306
  1306.2 269.4 %while.84 = (s32[]{:T(128)}, f32[32,512,3072]{2,1,0:T(8,128)}, s32[32]{0:T(128)S(1)}, bf16[32,40,512]{2,1,0:T(8,128)(2,1)}, bf16[32,40,1024]{2,1,0:T(8,128)(2,1)...) while((s32[]{:T(128)}, f32[32,512,3072]{2,1,0:T(8,128)}, ...), condition=%wide.region_44.45_spmd, body=%wide.region_43.44_spmd.sunk | while | flops 128974864 | bytes 19246440 | solution.py:329
  1575.7 8.9 gather_fusion.1
  1584.6 4.6 fusion.112
  1589.3 9.9 gather_fusion.3
  1612.0 8.2 while.86
  1631.5 38.7 %all-reduce.4 = (f32[1024]{0:T(1024)S(1)}, f32[1024]{0:T(1024)S(1)}) all-reduce(f32[1024]{0:T(1024)S(1)} %get-tuple-element.782, f32[1024]{0:T(1024)S(1)} %get-tuple-element.780), channel_id=2, replica_groups=mesh['fsdp'=32] {'fsdp'}, use_global_device_ids=true, to_apply=%region_36.37.clone | all-reduce | flops 2048 | bytes 16384
  1673.6 1498.4 %reduce-scatter.14.cloned.1.call-done = f32[512,3072]{1,0:T(8,128)} async-done(((f32[16384,3072]{1,0:T(8,128)}), f32[512,3072]{1,0:T(8,128)}) %reduce-scatter.14.cloned.1.call-update) | async-done | bytes 6291472 | tf_op jit(solution)/shard_map/reduce_scatter | solution.py:332
  3171.9 5.8 fusion.161
  3177.7 130.1 %reduce-scatter.12.cloned.1.call-done = f32[32,32]{1,0:T(8,128)} async-done(((f32[1024,32]{1,0:T(8,128)}), f32[32,32]{1,0:T(8,128)}) %reduce-scatter.12.cloned.1.call-update) | async-done | bytes 4112 | tf_op jit(solution)/shard_map/reduce_scatter | solution.py:386
  3307.9 139.9 %reduce-scatter.10.cloned.1.call-done = f32[32,1024]{1,0:T(8,128)} async-done(((f32[1024,1024]{1,0:T(8,128)}), f32[32,1024]{1,0:T(8,128)}) %reduce-scatter.10.cloned.1.call-update) | async-done | bytes 131088 | tf_op jit(solution)/shard_map/reduce_scatter | solution.py:384
  3447.8 139.7 %reduce-scatter.8.cloned.1.call-done = f32[32,1024]{1,0:T(8,128)} async-done(((f32[1024,1024]{1,0:T(8,128)}), f32[32,1024]{1,0:T(8,128)}) %reduce-scatter.8.cloned.1.call-update) | async-done | bytes 131088 | tf_op jit(solution)/shard_map/reduce_scatter | solution.py:383
  3587.5 139.7 %reduce-scatter.6.cloned.1.call-done = f32[32,1024]{1,0:T(8,128)} async-done(((f32[1024,1024]{1,0:T(8,128)}), f32[32,1024]{1,0:T(8,128)}) %reduce-scatter.6.cloned.1.call-update) | async-done | bytes 131088 | tf_op jit(solution)/shard_map/reduce_scatter | solution.py:382
  (708 shorter events, 859.5 us)
Async XLA Ops:
  7.2 4.1 copy-start.7
  7.2 4.4 copy-start.12
  7.2 4.7 copy-start.13
  7.2 47.0 %copy-start.11 = (s32[48]{0:T(128)S(1)}, s32[48]{0:T(128)}, u32[]{:S(2)}) copy-start(s32[48]{0:T(128)} %param.30) | copy-start | bytes 580
  7.2 47.0 %copy-start.10 = (s32[48]{0:T(128)S(1)}, s32[48]{0:T(128)}, u32[]{:S(2)}) copy-start(s32[48]{0:T(128)} %param.29) | copy-start | bytes 580
  7.2 66.6 %copy-start.3 = (bf16[128,1024]{1,0:T(8,128)(2,1)S(1)}, bf16[128,1024]{1,0:T(8,128)(2,1)}, u32[]{:S(2)}) copy-start(bf16[128,1024]{1,0:T(8,128)(2,1)} %param.41) | copy-start | bytes 786436
  7.2 114.1 %all-gather.7.cloned.1.call-start = ((), (), s32[]{:S(2)}) async-start(), calls=%async_computation.5 | async-start | bytes 2162688 | tf_op jit(solution)/shard_map/all_gather | solution.py:168
  8.0 120.3 %all-gather.9.cloned.1.call-start = ((), (), s32[]{:S(2)}) async-start(), calls=%async_computation.6 | async-start | bytes 2162688 | tf_op jit(solution)/shard_map/all_gather | solution.py:167
  8.7 177.7 %all-gather.11.cloned.1.call-start = ((), (), s32[]{:S(2)}) async-start(), calls=%async_computation.7 | async-start | bytes 2162688 | tf_op jit(solution)/shard_map/all_gather | solution.py:169
  9.5 373.4 %all-gather.13.cloned.1.call-start = ((), (), s32[]{:S(2)}) async-start(), calls=%async_computation.8 | async-start | bytes 34603008 | tf_op jit(solution)/shard_map/all_gather | solution.py:214
  10.0 568.5 %all-gather.15.cloned.1.call-start = ((), (), s32[]{:S(2)}) async-start(), calls=%async_computation.9 | async-start | bytes 34603008 | tf_op jit(solution)/shard_map/all_gather | solution.py:215
  10.6 763.6 %all-gather.17.cloned.1.call-start = ((), (), s32[]{:S(2)}) async-start(), calls=%async_computation.10 | async-start | bytes 34603008 | tf_op jit(solution)/shard_map/all_gather | solution.py:216
  11.2 3160.7 %reduce-scatter.14.cloned.1.call-start = ((), (), s32[]{:S(2)}) async-start(), calls=%async_computation.15 | async-start | bytes 207618048 | tf_op jit(solution)/shard_map/reduce_scatter | solution.py:332
  74.0 5.2 copy-start.9
  74.0 46.3 %copy-start = (bf16[128,1024]{1,0:T(8,128)(2,1)S(1)}, bf16[128,1024]{1,0:T(8,128)(2,1)}, u32[]{:S(2)}) copy-start(bf16[128,1024]{1,0:T(8,128)(2,1)} %param.28) | copy-start | bytes 786436
  779.0 3.0 copy-start.8
  1575.6 1732.2 %reduce-scatter.12.cloned.1.call-start = ((), (), s32[]{:S(2)}) async-start(), calls=%async_computation.14 | async-start | bytes 540672 | tf_op jit(solution)/shard_map/reduce_scatter | solution.py:386
  1599.3 4.6 copy-start.4
  1603.4 2.2 copy-start.2
  1607.7 1840.1 %reduce-scatter.10.cloned.1.call-start = ((), (), s32[]{:S(2)}) async-start(), calls=%async_computation.13 | async-start | bytes 4325376 | tf_op jit(solution)/shard_map/reduce_scatter | solution.py:384
  1610.8 1.2 copy-start.6
  1610.8 1976.6 %reduce-scatter.8.cloned.1.call-start = ((), (), s32[]{:S(2)}) async-start(), calls=%async_computation.12 | async-start | bytes 4325376 | tf_op jit(solution)/shard_map/reduce_scatter | solution.py:383
  1623.4 2103.8 %reduce-scatter.6.cloned.1.call-start = ((), (), s32[]{:S(2)}) async-start(), calls=%async_computation.11 | async-start | bytes 4325376 | tf_op jit(solution)/shard_map/reduce_scatter | solution.py:382
  1626.7 3.1 copy-start.1
  (1 other events, 1.1 us)
Sparse Core Ops, SparseCore 0:
  10.9 59.1 all-gather.6
  73.0 55.2 all-gather.8
  131.2 55.2 all-gather.10
  189.1 193.6 all-gather.12
  385.5 192.9 all-gather.14
  581.2 192.9 all-gather.16
  1575.8 1596.1 reduce-scatter.13
  3174.7 133.0 reduce-scatter.11
  3310.8 136.9 reduce-scatter.9
  3450.6 136.8 reduce-scatter.7
  3590.4 136.7 reduce-scatter.5
where the time goes:
time: 3740 us; the launch traced here: 3730 us
  waiting for transfers between devices  2670 us (71%)
  matrix products  618 us (17%)
  other arithmetic  176 us (5%)
  blocking collectives  122 us (3%)
  local copies, waits for them, and re-layouts  105 us (3%)
    reduce_scatter x1, waiting for transfers between devices, body(): lax.psum_scatter(blocks.reshape(lax.axis_size('fsdp') * shard_rows, 3 * m...  1500 us
    all_gather x1, waiting for transfers between devices, body(): piece_down = lax.all_gather(down_weight, 'fsdp', axis=0, tiled=True)  196 us
    all_gather x1, waiting for transfers between devices, body(): piece_up = lax.all_gather(up_weight, 'fsdp', axis=0, tiled=True)  196 us
    all_gather x1, waiting for transfers between devices, body(): piece_gate = lax.all_gather(gate_weight, 'fsdp', axis=0, tiled=True)  177 us
    reduce_scatter x1, waiting for transfers between devices, body(): lax.psum_scatter(output_weight_grad, 'fsdp', scatter_dimension=0, tiled=T...  140 us
    reduce_scatter x1, waiting for transfers between devices, body(): lax.psum_scatter(query_grad, 'fsdp', scatter_dimension=0, tiled=True)  140 us
    reduce_scatter x1, waiting for transfers between devices, body(): lax.psum_scatter(keyvalue_grad, 'fsdp', scatter_dimension=0, tiled=True)  140 us
    reduce_scatter x1, waiting for transfers between devices, body(): lax.psum_scatter(router_grad, 'fsdp', scatter_dimension=0, tiled=True)  130 us
  transfers between devices with their start and end apart: 11, of which 10 were waited for; matrix products, arithmetic and copies ran while one was open for 3% of the time, Pallas kernels for 0%

commit v1 on v0

v1 whole, which is shorter than its diff:
```python
from functools import partial

import jax
import jax.numpy as jnp
from jax import lax
from jax.sharding import PartitionSpec as P

QUERY_HEADS = 16
KEY_VALUE_HEADS = 8
HEAD_WIDTH = 64
EXPERT_COUNT = 32
EXPERT_HIDDEN = 512
TOPK = 8
CAP = 40


EPS = 1e-06
ROPE_BASE = 10000.0


def layout(seq_lengths, seq_devices, device, count_of_rows):
    on_device = seq_devices == device
    lengths = jnp.where(on_device, seq_lengths, 0)
    starts = jnp.cumsum(lengths) - lengths
    filled_rows = jnp.sum(lengths)
    row_slots = jnp.arange(count_of_rows, dtype=jnp.int32)
    inside = (row_slots[:, None] >= starts[None, :]) & (
        row_slots[:, None] < (starts + lengths)[None, :]
    )
    live_rows = jnp.any(inside, axis=1)
    seq_count = seq_lengths.shape[0]
    numbers = jnp.arange(seq_count, dtype=jnp.int32)
    segment = jnp.where(
        live_rows, jnp.sum(jnp.where(inside, numbers[None, :], 0), axis=1), seq_count
    )
    begins = jnp.where(
        live_rows, jnp.sum(jnp.where(inside, starts[None, :], 0), axis=1), filled_rows
    )
    return (live_rows, segment, row_slots - begins)


def rope_tables(position, head_dim):
    half_dim = head_dim // 2
    inverse = ROPE_BASE ** (-(jnp.arange(half_dim, dtype=jnp.float32) * 2.0) / head_dim)
    angles = position.astype(jnp.float32)[:, None] * inverse[None, :]
    return (jnp.cos(angles)[:, None, :], jnp.sin(angles)[:, None, :])


def rotate(values, cosine, sine_part, head_dim):
    count_of_rows = values.shape[0]
    shaped = values.reshape(count_of_rows, -1, head_dim)
    half_dim = head_dim // 2
    first_half = shaped[..., :half_dim]
    second_half = shaped[..., half_dim:]
    turned = jnp.concatenate(
        [
            first_half * cosine - second_half * sine_part,
            second_half * cosine + first_half * sine_part,
        ],
        axis=-1,
    )
    return turned.reshape(count_of_rows, -1)


def norm_forward(hidden, gain_vec):
    inv_rms = lax.rsqrt(jnp.mean(hidden * hidden, axis=-1, keepdims=True) + EPS)
    unit_rows = hidden * inv_rms
    return (unit_rows * gain_vec.astype(jnp.float32), unit_rows, inv_rms)


def norm_backward(grad_norm, gain_vec, unit_rows, inv_rms):
    grad_unit = grad_norm * gain_vec.astype(jnp.float32)
    grad_gain = jnp.sum(grad_norm * unit_rows, axis=0)
    grad_hidden = inv_rms * (
        grad_unit - unit_rows * jnp.mean(grad_unit * unit_rows, axis=-1, keepdims=True)
    )
    return (grad_hidden, grad_gain)


def head_forward(operands, allowed):
    query_rows, keys_head, values_head = operands
    scale_factor = query_rows.shape[-1] ** (-0.5)
    scores = (
        jnp.einsum("qgd,kd->gqk", query_rows, keys_head, preferred_element_type=jnp.float32)
        * scale_factor
    )
    scores = jnp.where(allowed[None], scores, -jnp.inf)
    highest = jnp.max(scores, axis=-1, keepdims=True)
    totals = jnp.sum(jnp.exp(scores - highest), axis=-1, keepdims=True)
    log_total = highest + jnp.log(totals)
    prob_bf = jnp.exp(scores - log_total).astype(jnp.bfloat16)
    mixed_out = jnp.einsum(
        "gqk,kd->qgd", prob_bf, values_head, preferred_element_type=jnp.float32
    ).astype(jnp.bfloat16)
    return (mixed_out, log_total[..., 0])


def head_backward(operands, allowed):
    query_rows, keys_head, values_head, mixed_out, grad_mixed, log_total = operands
    scale_factor = query_rows.shape[-1] ** (-0.5)
    scores = (
        jnp.einsum("qgd,kd->gqk", query_rows, keys_head, preferred_element_type=jnp.float32)
        * scale_factor
    )
    prob_full = jnp.where(allowed[None], jnp.exp(scores - log_total[..., None]), 0.0)
    prob_bf = prob_full.astype(jnp.bfloat16)
    grad_values = jnp.einsum("gqk,qgd->kd", prob_bf, grad_mixed, preferred_element_type=jnp.float32)
    grad_probs = jnp.einsum(
        "qgd,kd->gqk", grad_mixed, values_head, preferred_element_type=jnp.float32
    )
    inner = jnp.sum(
        grad_mixed.astype(jnp.float32) * mixed_out.astype(jnp.float32), axis=-1
    ).transpose(1, 0)
    grad_scores = (prob_full * (grad_probs - inner[..., None])).astype(jnp.bfloat16)
    grad_queries = (
        jnp.einsum("gqk,kd->qgd", grad_scores, keys_head, preferred_element_type=jnp.float32)
        * scale_factor
    )
    grad_keys = (
        jnp.einsum("gqk,qgd->kd", grad_scores, query_rows, preferred_element_type=jnp.float32)
        * scale_factor
    )
    return (grad_queries, grad_keys, grad_values)


def peer_plan(device, count):
    if count != 32:
        return [device % 2 + 2 * i for i in range(count // 2)]
    core = device % 2
    first = jnp.where(core == 0, 4, 2)
    second = 6 - first
    plan = []
    for plane in range(4):
        base = device ^ (8 * plane)
        plan += [base, base ^ first, base ^ second, base ^ 6]
    return plan


def swap_perm(mask):
    return [(i, i ^ mask) for i in range(32)]


def core_perm(count):
    return [(i, i ^ 1) for i in range(count)]


def first_perm():
    return [(i, i ^ (4 if i % 2 == 0 else 2)) for i in range(32)]


def second_perm():
    return [(i, i ^ (2 if i % 2 == 0 else 4)) for i in range(32)]


def permute(value, perm):
    return lax.ppermute(value, "fsdp", perm)


def parity_groups(count):
    return [list(range(0, count, 2)), list(range(1, count, 2))]


def gather_peers(shard, count):
    if count != 32:
        whole = lax.all_gather(shard, "fsdp", axis=0, axis_index_groups=parity_groups(count))
        return [whole[i] for i in range(count // 2)]
    rows = shard.shape[0]
    base = shard
    first_own = permute(base, first_perm())
    second_own = permute(base, second_perm())
    base_one = permute(base, swap_perm(8))
    base_two = permute(base, swap_perm(16))
    base_three = permute(base, swap_perm(24))
    across_own = permute(first_own, second_perm())
    second_one = permute(base_one, second_perm())
    first_one = permute(first_own, swap_perm(8))
    across_one = permute(across_own, swap_perm(8))
    far = jnp.concatenate([base_two, base_three], axis=0)
    first_far = permute(far, first_perm())
    second_far = permute(far, second_perm())
    across_far = permute(first_far, second_perm())
    return [
        base, first_own, second_own, across_own,
        base_one, first_one, second_one, across_one,
        base_two, first_far[:rows], second_far[:rows], across_far[:rows],
        base_three, first_far[rows:], second_far[rows:], across_far[rows:],
    ]


def add_wide(*terms):
    return sum(t.astype(jnp.float32) for t in terms)


def sum_to_peers(terms, count):
    if count != 32:
        stacked = jnp.concatenate([t.astype(jnp.float32) for t in terms], axis=0)
        return lax.psum_scatter(
            stacked, "fsdp", scatter_dimension=0, tiled=True, axis_index_groups=parity_groups(count)
        )
    bf = jnp.bfloat16
    rows = terms[0].shape[0]
    far = [jnp.concatenate([terms[8 + j], terms[12 + j]], axis=0) for j in range(4)]
    got = permute(far[3], second_perm())
    to_first = add_wide(far[1], got).astype(bf)
    got_first = permute(to_first, first_perm())
    got_second = permute(far[2], second_perm())
    base_far = add_wide(far[0], got_first, got_second).astype(bf)
    back_two = permute(base_far[:rows], swap_perm(16))
    back_three = permute(base_far[rows:], swap_perm(24))
    got_one = permute(terms[6], second_perm())
    base_one = add_wide(terms[4], got_one).astype(bf)
    back_one = permute(base_one, swap_perm(8))
    back_first = permute(terms[5], swap_perm(8))
    back_across = permute(terms[7], swap_perm(8))
    across = add_wide(terms[3], back_across).astype(bf)
    got_across = permute(across, second_perm())
    to_first = add_wide(terms[1], back_first, got_across).astype(bf)
    got_first = permute(to_first, first_perm())
    got_second = permute(terms[2], second_perm())
    return add_wide(terms[0], got_first, got_second, back_one, back_two, back_three)


def gather_dense(shard, device, count):
    if count != 32:
        return lax.all_gather(shard, "fsdp", axis=0, tiled=True)
    mine = jnp.stack(gather_peers(shard, count))
    theirs = permute(mine, core_perm(count))
    order = jnp.stack(peer_plan(device, count) + peer_plan(device ^ 1, count))
    place = jnp.zeros((count,), jnp.int32).at[order].set(jnp.arange(count, dtype=jnp.int32))
    both = jnp.concatenate([mine, theirs], axis=0)
    return both[place].reshape(count * shard.shape[0], -1)


def sum_dense(terms, device, count):
    if count != 32:
        return lax.psum_scatter(terms, "fsdp", scatter_dimension=0, tiled=True)[0]
    mine = terms[jnp.stack(peer_plan(device, count))]
    theirs = terms[jnp.stack(peer_plan(device ^ 1, count))].astype(jnp.bfloat16)
    both = (mine + permute(theirs, core_perm(count))).astype(jnp.bfloat16)
    return sum_to_peers([both[i] for i in range(count // 2)], count)


def expert_set(rows, cots, ids, router, tables, names):
    bf, f32 = jnp.bfloat16, jnp.float32
    dot = partial(jnp.einsum, preferred_element_type=f32)
    count_of_rows = rows.shape[1]
    logits = dot("btd,de->bte", rows, router)
    picker = jnp.any(ids[..., None] == jnp.arange(EXPERT_COUNT, dtype=jnp.int32), axis=2)
    raised = jnp.where(picker, jnp.exp(logits), 0.0)
    weights = raised / jnp.sum(raised, axis=-1, keepdims=True)
    out = jnp.zeros(rows.shape, f32)
    back = jnp.zeros(rows.shape, f32)
    route = jnp.zeros(rows.shape[:2] + (EXPERT_COUNT,), f32)
    grads = []
    for (gate, up, down), name in zip(tables, names):
        hit = jnp.any(ids == name, axis=2)
        rank = jnp.cumsum(hit.astype(jnp.int32), axis=1) - 1
        slots = jnp.arange(CAP, dtype=jnp.int32)
        chosen = hit[:, None, :] & (rank[:, None, :] == slots[None, :, None])
        pick = chosen.astype(bf)
        here = jnp.arange(EXPERT_COUNT, dtype=jnp.int32) == name
        weight = jnp.sum(jnp.where(here, weights, 0.0), axis=-1)
        slot_weight = jnp.sum(jnp.where(chosen, weight[:, None, :], 0.0), axis=-1)[..., None]
        inputs = dot("bst,btd->bsd", pick, rows).astype(bf)
        cot = dot("bst,btd->bsd", pick, cots)
        gate_pre = dot("bsd,hd->bsh", inputs, gate)
        up_pre = dot("bsd,hd->bsh", inputs, up)
        sigma = jax.nn.sigmoid(gate_pre)
        acts = (gate_pre * sigma * up_pre).astype(bf)
        result = dot("bsh,hd->bsd", acts, down)
        slot_route = jnp.sum(cot * result, axis=-1)
        pair_cot = (slot_weight * cot).astype(bf)
        act_grad = dot("bsd,hd->bsh", pair_cot, down)
        gate_pre_grad = (act_grad * up_pre * sigma * (1.0 + gate_pre * (1.0 - sigma))).astype(bf)
        up_pre_grad = (act_grad * gate_pre * sigma).astype(bf)
        in_grad = dot("bsh,hd->bsd", gate_pre_grad, gate) + dot("bsh,hd->bsd", up_pre_grad, up)
        grads.append(
            (
                dot("bsh,bsd->hd", gate_pre_grad, inputs),
                dot("bsh,bsd->hd", up_pre_grad, inputs),
                dot("bsh,bsd->hd", acts, pair_cot),
            )
        )
        out = out + dot("bst,bsd->btd", pick, (slot_weight * result).astype(bf))
        back = back + dot("bst,bsd->btd", pick, in_grad.astype(bf))
        row_route = jnp.sum(jnp.where(chosen, slot_route[..., None], 0.0), axis=1)
        route = route + jnp.where(here, row_route[..., None], 0.0)
    return (out.astype(bf), back.astype(bf), route, grads)


def body(
    block_input,
    seq_lengths,
    seq_devices,
    expert_ids,
    attn_gain,
    query_weight,
    keyvalue_weight,
    output_weight,
    moe_gain,
    router_weight,
    gate_weight,
    up_weight,
    down_weight,
    output_grad,
):
    bf, f32 = jnp.bfloat16, jnp.float32
    count_of_rows, model_width = block_input.shape
    device = lax.axis_index("fsdp").astype(jnp.int32)
    count = lax.axis_size("fsdp")
    shard_rows = gate_weight.shape[0]
    part = query_weight.shape[0]
    query_group_width = QUERY_HEADS // KEY_VALUE_HEADS
    key_value_columns = KEY_VALUE_HEADS * HEAD_WIDTH
    live_rows, segment, position = layout(seq_lengths, seq_devices, device, count_of_rows)
    live_col = live_rows[:, None]
    row_slots = jnp.arange(count_of_rows, dtype=jnp.int32)
    allowed = (segment[:, None] == segment[None, :]) & (row_slots[:, None] >= row_slots[None, :])
    cosine, sine_part = rope_tables(position, HEAD_WIDTH)

    small = jnp.concatenate([router_weight.reshape(-1), attn_gain, moe_gain])
    small_rows = -(-small.shape[0] // (16 * model_width)) * 16
    small = jnp.pad(small, (0, small_rows * model_width - small.shape[0])).reshape(small_rows, model_width)
    dense = gather_dense(jnp.concatenate([query_weight, keyvalue_weight, small], axis=0), device, count)
    dense = dense.reshape(count, -1, model_width)
    full_query = dense[:, :part].reshape(-1, model_width)
    full_kv = dense[:, part : 2 * part].reshape(-1, model_width)
    small = dense[:, 2 * part :].reshape(count, -1)
    full_router = small[:, : part * EXPERT_COUNT].reshape(-1, EXPERT_COUNT)
    full_gain1 = small[:, part * EXPERT_COUNT : part * EXPERT_COUNT + part].reshape(-1)
    full_gain2 = small[:, part * EXPERT_COUNT + part : part * EXPERT_COUNT + 2 * part].reshape(-1)
    full_out = gather_dense(output_weight, device, count)

    own_tables = jnp.stack([gate_weight, up_weight, down_weight])
    sibling_tables = permute(own_tables, core_perm(count))
    own_name = device * shard_rows // EXPERT_HIDDEN
    sibling_name = (device ^ 1) * shard_rows // EXPERT_HIDDEN

    masked_grad = jnp.where(live_col, output_grad, jnp.zeros((), bf))
    id_rows = expert_ids.astype(bf).reshape(-1, model_width)
    id_rows = jnp.pad(id_rows, ((0, -id_rows.shape[0] % 16), (0, 0)))
    cot_blocks = gather_peers(jnp.concatenate([masked_grad, id_rows], axis=0), count)

    input_f = block_input.astype(f32)
    attn_norm, attn_unit, attn_rms = norm_forward(input_f, full_gain1)
    attn_in = attn_norm.astype(bf)
    query_pre = jnp.dot(attn_in, full_query, preferred_element_type=f32)
    kv_pre = jnp.dot(attn_in, full_kv, preferred_element_type=f32)
    query_rows = rotate(query_pre, cosine, sine_part, HEAD_WIDTH).astype(bf)
    gathered_keys = rotate(kv_pre[:, :key_value_columns], cosine, sine_part, HEAD_WIDTH).astype(bf)
    gathered_values = kv_pre[:, key_value_columns:].astype(bf)
    query_head_rows = query_rows.reshape(
        count_of_rows, KEY_VALUE_HEADS, query_group_width, HEAD_WIDTH
    ).transpose(1, 0, 2, 3)
    key_head_rows = gathered_keys.reshape(count_of_rows, KEY_VALUE_HEADS, HEAD_WIDTH).transpose(1, 0, 2)
    value_head_rows = gathered_values.reshape(count_of_rows, KEY_VALUE_HEADS, HEAD_WIDTH).transpose(1, 0, 2)
    mixed_heads, log_totals = jax.vmap(partial(head_forward, allowed=allowed))(
        (query_head_rows, key_head_rows, value_head_rows)
    )
    attn_heads = mixed_heads.transpose(1, 0, 2, 3).reshape(count_of_rows, QUERY_HEADS * HEAD_WIDTH)
    residual = input_f + jnp.dot(attn_heads, full_out, preferred_element_type=f32)
    moe_norm, moe_unit, moe_rms = norm_forward(residual, full_gain2)
    moe_in = moe_norm.astype(bf)

    moe_blocks = gather_peers(moe_in, count)
    outs, backs, sums = [], [], None
    tables = [tuple(own_tables), tuple(sibling_tables)]
    step = len(moe_blocks) // 4
    for first in range(0, len(moe_blocks), step):
        cots = jnp.stack(cot_blocks[first : first + step])
        ids = cots[:, count_of_rows:].reshape(step, -1)[:, : count_of_rows * TOPK]
        ids = ids.reshape(step, count_of_rows, TOPK).astype(jnp.int32)
        out, back, route, grads = expert_set(
            jnp.stack(moe_blocks[first : first + step]),
            cots[:, :count_of_rows],
            ids,
            full_router,
            tables,
            [own_name, sibling_name],
        )
        high = route.astype(bf)
        low = (route - high.astype(f32)).astype(bf)
        packed = jnp.concatenate([high, low], axis=-1).reshape(step, -1, model_width)
        back = jnp.concatenate([back, packed], axis=1)
        outs += [out[i] for i in range(step)]
        backs += [back[i] for i in range(step)]
        sums = grads if sums is None else jax.tree.map(jnp.add, sums, grads)
    from_sibling = permute(jnp.stack(sums[1]), core_perm(count))
    gate_grad, up_grad, down_grad = [a + b for a, b in zip(sums[0], from_sibling)]

    back_sum = sum_to_peers(backs, count)
    slot_in_grad = back_sum[:count_of_rows]
    route = back_sum[count_of_rows:].reshape(count_of_rows, 2, EXPERT_COUNT)
    route_grad = route[:, 0] + route[:, 1]
    logits = jnp.dot(moe_in, full_router, preferred_element_type=f32)
    picker = jnp.any(expert_ids[..., None] == jnp.arange(EXPERT_COUNT, dtype=jnp.int32), axis=1)
    raised = jnp.where(picker, jnp.exp(logits), 0.0)
    route_weights = raised / jnp.sum(raised, axis=-1, keepdims=True)
    logit_grad = route_weights * (route_grad - jnp.sum(route_weights * route_grad, axis=-1, keepdims=True))
    logit_grad = logit_grad.astype(bf)

    moe_out = sum_to_peers(outs, count)
    block_output = jnp.where(live_col, residual + moe_out, 0.0).astype(bf)
    out_cot = masked_grad.astype(f32)
    moe_in_grad = slot_in_grad + jnp.einsum(
        "te,de->td", logit_grad, full_router, preferred_element_type=f32
    )
    router_grad = jnp.einsum("td,te->de", moe_in, logit_grad, preferred_element_type=f32)
    resid_part, moe_gain_grad = norm_backward(moe_in_grad, full_gain2, moe_unit, moe_rms)
    residual_grad = out_cot + resid_part
    residual_bf = residual_grad.astype(bf)
    output_weight_grad = jnp.einsum("tf,td->fd", attn_heads, residual_bf, preferred_element_type=f32)
    gradient_per_head = jnp.einsum(
        "td,fd->tf", residual_bf, full_out, preferred_element_type=f32
    ).astype(bf)
    head_gradients = gradient_per_head.reshape(
        count_of_rows, KEY_VALUE_HEADS, query_group_width, HEAD_WIDTH
    ).transpose(1, 0, 2, 3)
    grad_q, grad_k, grad_v = jax.vmap(partial(head_backward, allowed=allowed))(
        (query_head_rows, key_head_rows, value_head_rows, mixed_heads, head_gradients, log_totals)
    )
    query_rot_grad = grad_q.transpose(1, 0, 2, 3).reshape(count_of_rows, QUERY_HEADS * HEAD_WIDTH)
    key_rot_grad = grad_k.transpose(1, 0, 2).reshape(count_of_rows, key_value_columns)
    value_grad = grad_v.transpose(1, 0, 2).reshape(count_of_rows, key_value_columns)
    query_pre_grad = rotate(query_rot_grad, cosine, -sine_part, HEAD_WIDTH).astype(bf)
    kv_pre_grad = jnp.concatenate(
        [rotate(key_rot_grad, cosine, -sine_part, HEAD_WIDTH), value_grad], axis=1
    ).astype(bf)
    query_grad = jnp.einsum("td,tf->df", attn_in, query_pre_grad, preferred_element_type=f32)
    keyvalue_grad = jnp.einsum("td,tf->df", attn_in, kv_pre_grad, preferred_element_type=f32)
    attn_in_grad = jnp.einsum(
        "tf,df->td", query_pre_grad, full_query, preferred_element_type=f32
    ) + jnp.einsum("tf,df->td", kv_pre_grad, full_kv, preferred_element_type=f32)
    input_part, attn_gain_grad = norm_backward(attn_in_grad, full_gain1, attn_unit, attn_rms)
    input_grad = jnp.where(live_col, residual_grad + input_part, 0.0)

    def per_device(whole):
        return whole.reshape(count, part, -1)

    small_terms = jnp.concatenate(
        [
            router_grad.reshape(count, -1),
            attn_gain_grad.reshape(count, -1),
            moe_gain_grad.reshape(count, -1),
        ],
        axis=1,
    )
    small_terms = jnp.pad(small_terms, ((0, 0), (0, small_rows * model_width - small_terms.shape[1])))
    small_terms = small_terms.reshape(count, small_rows, model_width)
    dense_sum = sum_dense(
        jnp.concatenate(
            [per_device(query_grad), per_device(keyvalue_grad), per_device(output_weight_grad), small_terms],
            axis=1,
        ),
        device,
        count,
    )
    small_sum = dense_sum[3 * part :].reshape(-1)
    routers = part * EXPERT_COUNT
    return (
        block_output,
        input_grad,
        small_sum[routers : routers + part],
        dense_sum[:part],
        dense_sum[part : 2 * part],
        dense_sum[2 * part : 3 * part],
        small_sum[routers + part : routers + 2 * part],
        small_sum[:routers].reshape(part, EXPERT_COUNT),
        gate_grad,
        up_grad,
        down_grad,
    )


def solution(mesh):
    placed = (
        P("fsdp", None),
        P(),
        P(),
        P("fsdp", None),
        P("fsdp"),
        P("fsdp", None),
        P("fsdp", None),
        P("fsdp", None),
        P("fsdp"),
        P("fsdp", None),
        P("fsdp", None),
        P("fsdp", None),
        P("fsdp", None),
        P("fsdp", None),
    )
    return jax.shard_map(
        body,
        mesh=mesh,
        in_specs=placed,
        out_specs=(
            P("fsdp", None),
            P("fsdp", None),
            P("fsdp"),
            P("fsdp", None),
            P("fsdp", None),
            P("fsdp", None),
            P("fsdp"),
            P("fsdp", None),
            P("fsdp", None),
            P("fsdp", None),
            P("fsdp", None),
        ),
        check_vma=False,
    )
```

time: 3740 us -> 716 us (0.19)
  waiting for transfers between devices: 2670 us -> 154 us
  matrix products: 618 us -> 214 us
  blocking collectives: 122 us -> 0 us
  starting transfers between devices: 0.65 us -> 99.8 us
  other arithmetic: 176 us -> 86 us
  local copies, waits for them, and re-layouts: 105 us -> 146 us
    reduce_scatter x5 -> x0, waiting for transfers between devices: 2050 us -> none  [the longest x1 1500 us: body(): lax.psum_scatter(blocks.reshape(lax.axis_size('fsdp') * shard_rows, 3 * m...]
    all_gather x6 -> x0, waiting for transfers between devices: 623 us -> none  [the longest x1 196 us: body(): piece_down = lax.all_gather(down_weight, 'fsdp', axis=0, tiled=True)]
    dot_general x308 -> x108, matrix products: 609 us -> 201 us  [the longest x8 25.4 us: expert_set(): back = back + dot('bst,bsd->btd', pick, in_grad.astype(bf))]
    ppermute x0 -> x89, waiting for transfers between devices: none -> 154 us  [permute(): return lax.ppermute(value, 'fsdp', perm)]
    ppermute x0 -> x89, starting transfers between devices: none -> 99.8 us  [permute(): return lax.ppermute(value, 'fsdp', perm)]
    dynamic_update_slice x40 -> x0, other arithmetic: 97.5 us -> none  [the longest x32 97.4 us: body(): lax.map(one_term, jnp.arange(lax.axis_size('fsdp') * shard_rows // shard_...]
    unnamed x2 -> x0, blocking collectives: 80.8 us -> none
    unnamed x35 -> x638, local copies, waits for them, and re-layouts: 3.56 us -> 54.9 us
  transfers between devices with their start and end apart: 11 -> 89, of which waited for: 10 -> 35; matrix products, arithmetic and copies ran while one was open for 3% -> 40% of each run, Pallas kernels for 0% -> 0%
where the time goes in v1:
time: 716 us; the launch traced here: 703 us
  matrix products  214 us (30%)
  waiting for transfers between devices  154 us (22%)
  local copies, waits for them, and re-layouts  146 us (20%)
  starting transfers between devices  99.8 us (14%)
  other arithmetic  86 us (12%)
    ppermute x89, waiting for transfers between devices, permute(): return lax.ppermute(value, 'fsdp', perm)  154 us
    ppermute x89, starting transfers between devices, permute(): return lax.ppermute(value, 'fsdp', perm)  99.8 us
    unnamed x638, local copies, waits for them, and re-layouts  54.9 us
    dot_general x8, matrix products, expert_set(): back = back + dot('bst,bsd->btd', pick, in_grad.astype(bf))  25.4 us
    dot_general x8, matrix products, expert_set(): dot('bsh,bsd->hd', up_pre_grad, inputs)  19.8 us
    dot_general x8, matrix products, expert_set(): dot('bsh,bsd->hd', gate_pre_grad, inputs)  18.5 us
    dot_general x8, matrix products, expert_set(): dot('bsh,bsd->hd', acts, pair_cot)  17.7 us
    dot_general x8, matrix products, expert_set(): up_pre = dot('bsd,hd->bsh', inputs, up)  15.3 us
  transfers between devices with their start and end apart: 89, of which 35 were waited for; matrix products, arithmetic and copies ran while one was open for 40% of the time, Pallas kernels for 0%

profile of v1, /device:TPU:0, one launch (start us, length us, event | category | flops | bytes accessed | tf_op | source)
XLA Modules:
  0.0 703.2 jit_solution(7962997600923160355)
XLA Ops:
  39.2 5.0 collective-permute-done.20
  44.2 6.1 collective-permute-done.21
  59.7 5.5 collective-permute-done.17
  80.3 4.9 collective-permute-start.19
  150.3 6.0 collective-permute-done.11
  197.8 5.9 gather_fusion
  203.6 5.0 fusion.368
  216.8 4.3 copy.72
  245.5 11.6 %collective-permute-done.53 = bf16[128,1024]{1,0:T(8,128)(2,1)} collective-permute-done((bf16[128,1024]{1,0:T(8,128)(2,1)}, bf16[128,1024]{1,0:T(8,128)(2,1)}, u32[]{:S(2)}, u32[]{:S(2)}) %collective-permute-start.53) | collective-permute-done | bytes 262176 | tf_op jit(solution)/shard_map/ppermute | solution.py:156
  387.3 3.9 add_convert_fusion.1
  460.9 4.8 fusion.8
  486.6 4.0 collective-permute-done.41
  496.2 4.0 collective-permute-done.65
  508.7 8.7 %collective-permute-done.60 = bf16[256,1024]{1,0:T(8,128)(2,1)S(1)} collective-permute-done((bf16[256,1024]{1,0:T(8,128)(2,1)S(1)}, bf16[256,1024]{1,0:T(8,128)(2,1)S(1)}, u32[]{:S(2)}, u32[]{:S(2)}) %collective-permute-start.60) | collective-permute-done | bytes 524320 | tf_op jit(solution)/shard_map/ppermute | solution.py:156
  530.5 16.9 %collective-permute-done.73 = bf16[136,1024]{1,0:T(8,128)(2,1)S(1)} collective-permute-done((bf16[136,1024]{1,0:T(8,128)(2,1)S(1)}, bf16[136,1024]{1,0:T(8,128)(2,1)S(1)}, u32[]{:S(2)}, u32[]{:S(2)}) %collective-permute-start.73) | collective-permute-done | bytes 278560 | tf_op jit(solution)/shard_map/ppermute | solution.py:156
  549.1 7.0 collective-permute-done.61
  583.3 7.8 %pad_maximum_fusion = f32[32,112,1024]{2,1,0:T(8,128)} fusion(f32[32,16,1024]{2,1,0:T(8,128)S(1)} %bitcast.832, f32[32,32,1024]{2,1,0:T(8,128)} %fusion.180, f32[32,32,1024]{2,1,0:T(8,128)S(1)} %bitcast.831, f32[32,32,1024]{2,1,0:T(8,128)S(1)} %fusion.384), kind=kLoop, calls=%fused_computation.9 | loop fusion | flops 11010048 | bytes 29360128 | tf_op jit(solution)/shard_map/concatenate | solution.py:451
  591.1 8.0 %gather_fusion.3 = bf16[16,112,1024]{2,1,0:T(8,128)(2,1)} fusion(f32[32,112,1024]{2,1,0:T(8,128)} %pad_maximum_fusion, s32[1024]{0:T(1024)} %pad_clamp_fusion), kind=kCustom, calls=%fused_computation.3 | custom fusion | bytes 7340096 | tf_op jit(solution)/shard_map/gather | solution.py:238
  624.5 9.3 %gather_fusion.2 = f32[16,112,1024]{2,1,0:T(8,128)} fusion(f32[32,112,1024]{2,1,0:T(8,128)} %pad_maximum_fusion, s32[1024]{0:T(1024)} %pad_clamp_fusion.1), kind=kCustom, calls=%fused_computation.2 | custom fusion | bytes 14680128 | tf_op jit(solution)/shard_map/gather | solution.py:237
  633.8 5.5 add_convert_fusion
  657.0 4.2 collective-permute-done.78
  668.7 6.7 collective-permute-done.87
  675.4 12.0 %collective-permute-done.86 = bf16[112,1024]{1,0:T(8,128)(2,1)S(1)} collective-permute-done((bf16[112,1024]{1,0:T(8,128)(2,1)S(1)}, bf16[112,1024]{1,0:T(8,128)(2,1)S(1)}, u32[]{:S(2)}, u32[]{:S(2)}) %collective-permute-start.86) | collective-permute-done | bytes 229408 | tf_op jit(solution)/shard_map/ppermute | solution.py:156
  689.7 5.5 fusion.6
  (1118 shorter events, 536.5 us)
Async XLA Ops:
  6.6 64.2 %collective-permute-start = (bf16[80,1024]{1,0:T(8,128)(2,1)}, bf16[80,1024]{1,0:T(8,128)(2,1)}, u32[]{:S(2)}, u32[]{:S(2)}) collective-permute-start(bf16[80,1024]{1,0:T(8,128)(2,1)} %constant_dynamic-update-slice_fusion), channel_id=1, source_target_pairs={{0,4},{1,3},{2,6},{3,1},{4,0},{5,7},{6,2},{7,5},{8,12},{9,11},{10,... | collective-permute-start | bytes 491528 | tf_op jit(solution)/shard_map/ppermute | solution.py:156
  9.6 64.0 %collective-permute-start.1 = (bf16[80,1024]{1,0:T(8,128)(2,1)}, bf16[80,1024]{1,0:T(8,128)(2,1)}, u32[]{:S(2)}, u32[]{:S(2)}) collective-permute-start(bf16[80,1024]{1,0:T(8,128)(2,1)} %constant_dynamic-update-slice_fusion), channel_id=1, source_target_pairs={{0,2},{1,5},{2,0},{3,7},{4,6},{5,1},{6,4},{7,3},{8,10},{9,13},{10,... | collective-permute-start | bytes 491528 | tf_op jit(solution)/shard_map/ppermute | solution.py:156
  11.0 105.5 %collective-permute-start.3 = (bf16[80,1024]{1,0:T(8,128)(2,1)}, bf16[80,1024]{1,0:T(8,128)(2,1)}, u32[]{:S(2)}, u32[]{:S(2)}) collective-permute-start(bf16[80,1024]{1,0:T(8,128)(2,1)} %constant_dynamic-update-slice_fusion), channel_id=1, source_target_pairs={{0,8},{1,9},{2,10},{3,11},{4,12},{5,13},{6,14},{7,15},{8,0},{9,1},... | collective-permute-start | bytes 491528 | tf_op jit(solution)/shard_map/ppermute | solution.py:156
  12.6 65.3 %collective-permute-start.7 = (bf16[80,1024]{1,0:T(8,128)(2,1)}, bf16[80,1024]{1,0:T(8,128)(2,1)}, u32[]{:S(2)}, u32[]{:S(2)}) collective-permute-start(bf16[80,1024]{1,0:T(8,128)(2,1)} %constant_dynamic-update-slice_fusion), channel_id=1, source_target_pairs={{0,16},{1,17},{2,18},{3,19},{4,20},{5,21},{6,22},{7,23},{8,24},{9,... | collective-permute-start | bytes 491528 | tf_op jit(solution)/shard_map/ppermute | solution.py:156
  70.8 31.6 %collective-permute-start.48 = (bf16[144,1024]{1,0:T(8,128)(2,1)S(1)}, bf16[144,1024]{1,0:T(8,128)(2,1)S(1)}, u32[]{:S(2)}, u32[]{:S(2)}) collective-permute-start(bf16[144,1024]{1,0:T(8,128)(2,1)S(1)} %copy-done.128), channel_id=1, source_target_pairs={{0,16},{1,17},{2,18},{3,19},{4,20},{5,21},{6,22},{7,23},{8,24},{9,... | collective-permute-start | bytes 884744 | tf_op jit(solution)/shard_map/ppermute | solution.py:156
  73.6 29.9 %collective-permute-start.49 = (bf16[144,1024]{1,0:T(8,128)(2,1)S(1)}, bf16[144,1024]{1,0:T(8,128)(2,1)S(1)}, u32[]{:S(2)}, u32[]{:S(2)}) collective-permute-start(bf16[144,1024]{1,0:T(8,128)(2,1)S(1)} %copy-done.128), channel_id=1, source_target_pairs={{0,24},{1,25},{2,26},{3,27},{4,28},{5,29},{6,30},{7,31},{8,16},{9,... | collective-permute-start | bytes 884744 | tf_op jit(solution)/shard_map/ppermute | solution.py:156
  77.9 57.8 %collective-permute-start.26 = (bf16[144,1024]{1,0:T(8,128)(2,1)S(1)}, bf16[144,1024]{1,0:T(8,128)(2,1)}, u32[]{:S(2)}, u32[]{:S(2)}) collective-permute-start(bf16[144,1024]{1,0:T(8,128)(2,1)S(1)} %copy-done.128), channel_id=1, source_target_pairs={{0,4},{1,3},{2,6},{3,1},{4,0},{5,7},{6,2},{7,5},{8,12},{9,11},{10,... | collective-permute-start | bytes 884744 | tf_op jit(solution)/shard_map/ppermute | solution.py:156
  100.0 41.2 %collective-permute-start.27 = (bf16[144,1024]{1,0:T(8,128)(2,1)S(1)}, bf16[144,1024]{1,0:T(8,128)(2,1)S(1)}, u32[]{:S(2)}, u32[]{:S(2)}) collective-permute-start(bf16[144,1024]{1,0:T(8,128)(2,1)S(1)} %copy-done.128), channel_id=1, source_target_pairs={{0,2},{1,5},{2,0},{3,7},{4,6},{5,1},{6,4},{7,3},{8,10},{9,13},{10,... | collective-permute-start | bytes 884744 | tf_op jit(solution)/shard_map/ppermute | solution.py:156
  103.5 39.7 %collective-permute-start.33 = (bf16[144,1024]{1,0:T(8,128)(2,1)S(1)}, bf16[144,1024]{1,0:T(8,128)(2,1)}, u32[]{:S(2)}, u32[]{:S(2)}) collective-permute-start(bf16[144,1024]{1,0:T(8,128)(2,1)S(1)} %copy-done.128), channel_id=1, source_target_pairs={{0,8},{1,9},{2,10},{3,11},{4,12},{5,13},{6,14},{7,15},{8,0},{9,1},... | collective-permute-start | bytes 884744 | tf_op jit(solution)/shard_map/ppermute | solution.py:156
  135.7 139.0 %collective-permute-start.32 = (bf16[3,512,1024]{2,1,0:T(8,128)(2,1)}, bf16[3,512,1024]{2,1,0:T(8,128)(2,1)}, u32[]{:S(2)}, u32[]{:S(2)}) collective-permute-start(bf16[3,512,1024]{2,1,0:T(8,128)(2,1)} %pad_maximum_fusion.2), channel_id=1, source_target_pairs={{0,1},{1,0},{2,3},{3,2},{4,5},{5,4},{6,7},{7,6},{8,9},{9,8},{10,11... | collective-permute-start | bytes 9437192 | tf_op jit(solution)/shard_map/ppermute | solution.py:156
  140.0 30.5 %collective-permute-start.50 = (bf16[288,1024]{1,0:T(8,128)(2,1)}, bf16[288,1024]{1,0:T(8,128)(2,1)}, u32[]{:S(2)}, u32[]{:S(2)}) collective-permute-start(bf16[288,1024]{1,0:T(8,128)(2,1)} %constant_dynamic-update-slice_fusion.53), channel_id=1, source_target_pairs={{0,4},{1,3},{2,6},{3,1},{4,0},{5,7},{6,2},{7,5},{8,12},{9,11},{10,... | collective-permute-start | bytes 1769480 | tf_op jit(solution)/shard_map/ppermute | solution.py:156
  264.8 27.3 %collective-permute-start.56 = (bf16[256,1024]{1,0:T(8,128)(2,1)}, bf16[256,1024]{1,0:T(8,128)(2,1)}, u32[]{:S(2)}, u32[]{:S(2)}) collective-permute-start(bf16[256,1024]{1,0:T(8,128)(2,1)} %constant_dynamic-update-slice_fusion.55), channel_id=1, source_target_pairs={{0,2},{1,5},{2,0},{3,7},{4,6},{5,1},{6,4},{7,3},{8,10},{9,13},{10,... | collective-permute-start | bytes 1572872 | tf_op jit(solution)/shard_map/ppermute | solution.py:156
  265.8 28.2 %collective-permute-start.38 = (bf16[128,1024]{1,0:T(8,128)(2,1)}, bf16[128,1024]{1,0:T(8,128)(2,1)}, u32[]{:S(2)}, u32[]{:S(2)}) collective-permute-start(bf16[128,1024]{1,0:T(8,128)(2,1)} %collective-permute-done.29), channel_id=1, source_target_pairs={{0,8},{1,9},{2,10},{3,11},{4,12},{5,13},{6,14},{7,15},{8,0},{9,1},... | collective-permute-start | bytes 786440 | tf_op jit(solution)/shard_map/ppermute | solution.py:156
  406.2 95.4 %collective-permute-start.72 = (bf16[272,1024]{1,0:T(8,128)(2,1)}, bf16[272,1024]{1,0:T(8,128)(2,1)}, u32[]{:S(2)}, u32[]{:S(2)}) collective-permute-start(bf16[272,1024]{1,0:T(8,128)(2,1)} %pad_maximum_fusion.20), channel_id=1, source_target_pairs={{0,2},{1,5},{2,0},{3,7},{4,6},{5,1},{6,4},{7,3},{8,10},{9,13},{10,... | collective-permute-start | bytes 1671176 | tf_op jit(solution)/shard_map/ppermute | solution.py:156
  408.2 76.0 %collective-permute-start.70 = (bf16[272,1024]{1,0:T(8,128)(2,1)}, bf16[272,1024]{1,0:T(8,128)(2,1)}, u32[]{:S(2)}, u32[]{:S(2)}) collective-permute-start(bf16[272,1024]{1,0:T(8,128)(2,1)} %pad_maximum_fusion.19), channel_id=1, source_target_pairs={{0,2},{1,5},{2,0},{3,7},{4,6},{5,1},{6,4},{7,3},{8,10},{9,13},{10,... | collective-permute-start | bytes 1671176 | tf_op jit(solution)/shard_map/ppermute | solution.py:156
  435.8 43.6 %collective-permute-start.68 = (bf16[136,1024]{1,0:T(8,128)(2,1)}, bf16[136,1024]{1,0:T(8,128)(2,1)}, u32[]{:S(2)}, u32[]{:S(2)}) collective-permute-start(bf16[136,1024]{1,0:T(8,128)(2,1)} %get-tuple-element.75), channel_id=1, source_target_pairs={{0,2},{1,5},{2,0},{3,7},{4,6},{5,1},{6,4},{7,3},{8,10},{9,13},{10,... | collective-permute-start | bytes 835592 | tf_op jit(solution)/shard_map/ppermute | solution.py:156
  446.3 28.1 %collective-permute-start.46 = (bf16[128,1024]{1,0:T(8,128)(2,1)}, bf16[128,1024]{1,0:T(8,128)(2,1)}, u32[]{:S(2)}, u32[]{:S(2)}) collective-permute-start(bf16[128,1024]{1,0:T(8,128)(2,1)} %get-tuple-element.85), channel_id=1, source_target_pairs={{0,2},{1,5},{2,0},{3,7},{4,6},{5,1},{6,4},{7,3},{8,10},{9,13},{10,... | collective-permute-start | bytes 786440 | tf_op jit(solution)/shard_map/ppermute | solution.py:156
  448.6 27.7 %collective-permute-start.42 = (bf16[128,1024]{1,0:T(8,128)(2,1)}, bf16[128,1024]{1,0:T(8,128)(2,1)}, u32[]{:S(2)}, u32[]{:S(2)}) collective-permute-start(bf16[128,1024]{1,0:T(8,128)(2,1)} %get-tuple-element.86), channel_id=1, source_target_pairs={{0,8},{1,9},{2,10},{3,11},{4,12},{5,13},{6,14},{7,15},{8,0},{9,1},... | collective-permute-start | bytes 786440 | tf_op jit(solution)/shard_map/ppermute | solution.py:156
  493.3 27.3 %collective-permute-start.67 = (bf16[136,1024]{1,0:T(8,128)(2,1)S(1)}, bf16[136,1024]{1,0:T(8,128)(2,1)S(1)}, u32[]{:S(2)}, u32[]{:S(2)}) collective-permute-start(bf16[136,1024]{1,0:T(8,128)(2,1)S(1)} %fusion.179), channel_id=1, source_target_pairs={{0,2},{1,5},{2,0},{3,7},{4,6},{5,1},{6,4},{7,3},{8,10},{9,13},{10,... | collective-permute-start | bytes 835592 | tf_op jit(solution)/shard_map/ppermute | solution.py:156
  519.1 28.3 %collective-permute-start.73 = (bf16[136,1024]{1,0:T(8,128)(2,1)S(1)}, bf16[136,1024]{1,0:T(8,128)(2,1)S(1)}, u32[]{:S(2)}, u32[]{:S(2)}) collective-permute-start(bf16[136,1024]{1,0:T(8,128)(2,1)S(1)} %get-tuple-element.121), channel_id=1, source_target_pairs={{0,16},{1,17},{2,18},{3,19},{4,20},{5,21},{6,22},{7,23},{8,24},{9,... | collective-permute-start | bytes 835592 | tf_op jit(solution)/shard_map/ppermute | solution.py:156
  520.7 28.4 %collective-permute-start.45 = (bf16[128,1024]{1,0:T(8,128)(2,1)}, bf16[128,1024]{1,0:T(8,128)(2,1)}, u32[]{:S(2)}, u32[]{:S(2)}) collective-permute-start(bf16[128,1024]{1,0:T(8,128)(2,1)} %slice_bitcast_fusion.28), channel_id=1, source_target_pairs={{0,2},{1,5},{2,0},{3,7},{4,6},{5,1},{6,4},{7,3},{8,10},{9,13},{10,... | collective-permute-start | bytes 786440 | tf_op jit(solution)/shard_map/ppermute | solution.py:156
  521.9 27.2 %collective-permute-start.47 = (bf16[128,1024]{1,0:T(8,128)(2,1)}, bf16[128,1024]{1,0:T(8,128)(2,1)}, u32[]{:S(2)}, u32[]{:S(2)}) collective-permute-start(bf16[128,1024]{1,0:T(8,128)(2,1)} %fusion.109), channel_id=1, source_target_pairs={{0,8},{1,9},{2,10},{3,11},{4,12},{5,13},{6,14},{7,15},{8,0},{9,1},... | collective-permute-start | bytes 786440 | tf_op jit(solution)/shard_map/ppermute | solution.py:156
  599.1 34.7 %collective-permute-start.75 = (bf16[16,112,1024]{2,1,0:T(8,128)(2,1)}, bf16[16,112,1024]{2,1,0:T(8,128)(2,1)}, u32[]{:S(2)}, u32[]{:S(2)}) collective-permute-start(bf16[16,112,1024]{2,1,0:T(8,128)(2,1)} %gather_fusion.3), channel_id=1, source_target_pairs={{0,1},{1,0},{2,3},{3,2},{4,5},{5,4},{6,7},{7,6},{8,9},{9,8},{10,11... | collective-permute-start | bytes 11010056 | tf_op jit(solution)/shard_map/ppermute | solution.py:156
  609.6 80.0 %collective-permute-start.88 = (f32[3,512,1024]{2,1,0:T(8,128)}, f32[3,512,1024]{2,1,0:T(8,128)}, u32[]{:S(2)}, u32[]{:S(2)}) collective-permute-start(f32[3,512,1024]{2,1,0:T(8,128)} %pad_maximum_fusion.1), channel_id=1, source_target_pairs={{0,1},{1,0},{2,3},{3,2},{4,5},{5,4},{6,7},{7,6},{8,9},{9,8},{10,11... | collective-permute-start | bytes 18874376 | tf_op jit(solution)/shard_map/ppermute | solution.py:156
  (362 other events, 2923.4 us)
